TPU v7x, 32 devices: a whole 2x2x4 slice. The times are simulated.
32 devices in a mesh: seq: 4 (over y, x), head: 8 (over z, core).
Axes of the slice: x: 2, y: 2, z: 4, core: 2. Of those that a mesh axis runs over, the one named last changes fastest.
Arguments:
- hidden_in: bfloat16 [2, 2048, 2048], P(None, ('seq', 'head')), may hold values from -6 to 6
- seq_starts: int32 [2, 4], replicated, may hold values from 0 to 2047, as said below
- norm_gain: bfloat16 [2048], P(('seq', 'head')), may hold values from 0.5 to 1.5
- in_weight: bfloat16 [2048, 8512], P(('seq', 'head')), may hold values from -0.125 to 0.125
- conv_weight: bfloat16 [4, 4352], P(None, ('seq', 'head')), may hold values from -3 to 3
- conv_bias: bfloat16 [4352], P(('seq', 'head')), may hold values from -3 to 3
- decay_log: float32 [64], P('head'), may hold values from -7 to 1
- dt_bias: float32 [64], P('head'), may hold values from -6 to -2
- skip_gain: float32 [64], P('head'), may hold values from 0.5 to 1.5
- gate_gain: bfloat16 [4096], P(('seq', 'head')), may hold values from 0.5 to 1.5
- out_weight: bfloat16 [4096, 2048], P(('seq', 'head')), may hold values from -0.09375 to 0.09375
- out_grad: bfloat16 [2, 2048, 2048], P(None, ('seq', 'head')), may hold values from -6 to 6
Outputs:
- hidden_out: bfloat16 [2, 2048, 2048], P(None, ('seq', 'head'))
- grad_in: bfloat16 [2, 2048, 2048], P(None, ('seq', 'head'))
- grad_norm_gain: float32 [2048], P(('seq', 'head'))
- grad_in_weight: float32 [2048, 8512], P(('seq', 'head'))
- grad_conv_weight: float32 [4, 4352], P(None, ('seq', 'head'))
- grad_conv_bias: float32 [4352], P(('seq', 'head'))
- grad_decay_log: float32 [64], P('head')
- grad_dt_bias: float32 [64], P('head')
- grad_skip_gain: float32 [64], P('head')
- grad_gate_gain: float32 [4096], P(('seq', 'head'))
- grad_out_weight: float32 [4096, 2048], P(('seq', 'head'))
Inputs may be any that keep to these rules, and one draw needn't show every extreme that they name: `seq_starts`: start offsets of the 4 sequences of each micro-batch: the first is 0 and they rise strictly.
All inputs are finite; a program needn't handle non-finite values.
Results may differ from a plain program's by a relative error of at most 0.0084.
Values may be sent and summed in bfloat16 or wider, within the bound.
No kernel may reach another device: no remote copies, remote signals or barrier semaphores. Data moves between devices by JAX's collectives and lax.ppermute only.
A program may use at most 448 MiB of HBM per device.

v0:
```python
import jax
import jax.numpy as jnp
from jax import lax
from jax.sharding import PartitionSpec as P

HEADS = 64
HEADDIM = 64
STATE = 128
CONV_K = 4
SCAN_BLOCK = 256
MICRO = 2
D_INNER = 4096
CONV_CH = 4352


precise = lax.Precision.HIGHEST
eps = 1e-05


def from_behind(x, axis, by):
    count = lax.axis_size(axis)
    pairs = [(i, i + by) for i in range(count) if 0 <= i + by < count]
    return lax.ppermute(x, axis, pairs)


def carried_in(x, axis, combine, identity):
    count, mine = (lax.axis_size(axis), lax.axis_index(axis))
    everything = jax.tree.map(lambda part: lax.all_gather(part, axis), x)
    start = jax.tree.map(
        lambda part, zero: jnp.broadcast_to(jnp.asarray(zero, part.dtype), part.shape), x, identity
    )

    def lap(k, before):
        reached = k < mine
        new = combine(before, jax.tree.map(lambda part: part[k], everything))
        return jax.tree.map(lambda a, b: jnp.where(reached, a, b), new, before)

    return lax.fori_loop(0, count, lap, start)


def carried_in_2(x, axis, join, neutral):
    count = lax.axis_size(axis)
    place = lax.axis_index(axis)
    ahead = count - 1 - place
    gathered = jax.tree.map(
        lambda a, kind: lax.all_gather(a.astype(kind), axis), x, (jnp.bfloat16, jnp.bfloat16)
    )
    state = jax.tree.map(lambda a, e: jnp.zeros_like(a) + jnp.asarray(e, a.dtype), x, neutral)

    def one(lap, state):
        source = count - 1 - lap
        return join(
            state,
            jax.tree.map(
                lambda a, own: lax.dynamic_index_in_dim(a, source, 0, False).astype(own.dtype),
                gathered,
                x,
            ),
        )

    return lax.fori_loop(0, ahead, one, state)


def seg_ids(starts, positions):
    hits = (starts[:, None, :] <= positions[None, :, None]).astype(jnp.int32)
    return jnp.sum(hits, axis=2) - 1


def start_flags(starts, positions):
    return jnp.sum((starts[:, None, :] == positions[None, :, None]).astype(jnp.float32), axis=2)


def normed_rows(inputs, gain):
    return inputs * lax.rsqrt(jnp.mean(inputs * inputs, axis=-1, keepdims=True) + eps) * gain


def gated_norm(mixer_in, gate_in, gain):
    gated = mixer_in * jax.nn.silu(gate_in)
    return gated * lax.rsqrt(jnp.mean(gated * gated, axis=-1, keepdims=True) + eps) * gain


def link_states(earlier, later):
    return (earlier[0] * later[0], later[0] * earlier[1] + later[1])


def block_scan(values, keys, step_raw, decay_log, dt_bias, skip_gain, segs, firsts):
    block_len, head_count, head_width = values.shape
    blocks_here = block_len // SCAN_BLOCK
    block_vals = values.reshape(blocks_here, SCAN_BLOCK, head_count, head_width)
    write_key = keys[:, :STATE].reshape(blocks_here, SCAN_BLOCK, STATE)
    read_key = keys[:, STATE:].reshape(blocks_here, SCAN_BLOCK, STATE)
    step_size = jax.nn.softplus(step_raw + dt_bias[None, :]).reshape(
        blocks_here, SCAN_BLOCK, head_count
    )
    log_decay = jnp.cumsum(step_size * (-jnp.exp(decay_log))[None, None, :], axis=1)
    seg_blocks = segs.reshape(blocks_here, SCAN_BLOCK)
    first_blocks = firsts.reshape(blocks_here, SCAN_BLOCK)
    causal = jnp.arange(SCAN_BLOCK)[:, None] >= jnp.arange(SCAN_BLOCK)[None, :]
    same_seq = ((seg_blocks[:, :, None] == seg_blocks[:, None, :]) & causal[None])[..., None]
    spread = log_decay[:, :, None, :] - log_decay[:, None, :, :]
    within = jnp.where(same_seq, jnp.exp(jnp.where(same_seq, spread, 0.0)), 0.0)
    scores = jnp.einsum("nqk,nsk->nqs", read_key, write_key, precision=precise)
    weights = scores[..., None] * within * step_size[:, None, :, :]
    result = jnp.einsum("nqsh,nshp->nqhp", weights, block_vals, precision=precise)
    open_seq = (jnp.cumsum(first_blocks, axis=1) == 0)[..., None]
    carry_in = jnp.where(open_seq, jnp.exp(log_decay), 0.0)
    tail_seq = (seg_blocks == seg_blocks[:, -1:])[..., None]
    to_end = jnp.where(
        tail_seq, jnp.exp(jnp.where(tail_seq, log_decay[:, -1:, :] - log_decay, 0.0)), 0.0
    )
    block_state = jnp.einsum(
        "nsh,nshp,nsk->nhpk", to_end * step_size, block_vals, write_key, precision=precise
    )
    block_decay = jnp.where(open_seq[:, -1, :], jnp.exp(log_decay[:, -1, :]), 0.0)

    def advance(carried, inputs_now):
        state_now, reach_now = carried
        part_state, part_decay = inputs_now
        return (
            (part_decay[:, None, None] * state_now + part_state, part_decay * reach_now),
            (state_now, reach_now),
        )

    zero_state = jnp.zeros((head_count, head_width, STATE), jnp.float32)
    (dev_state, dev_decay), (before, prefix) = lax.scan(
        advance, (zero_state, jnp.ones((head_count,), jnp.float32)), (block_state, block_decay)
    )
    result = result + carry_in[..., None] * jnp.einsum(
        "nqk,nhpk->nqhp", read_key, before, precision=precise
    )
    result = result + skip_gain[None, None, :, None] * block_vals
    reach_all = (carry_in * prefix[:, None, :]).reshape(block_len, head_count)
    return (result.reshape(block_len, head_count, head_width), dev_decay, dev_state, reach_all)


def body(
    hidden_in,
    seq_starts,
    norm_gain,
    in_weight,
    conv_weight,
    conv_bias,
    decay_log,
    dt_bias,
    skip_gain,
    gate_gain,
    out_weight,
    out_grad,
):
    gain_all, in_all, conv_all, bias_all, gate_all, out_all = (
        lax.all_gather(norm_gain, ("seq", "head"), axis=0, tiled=True),
        lax.all_gather(in_weight, ("seq", "head"), axis=0, tiled=True),
        lax.all_gather(conv_weight, ("seq", "head"), axis=1, tiled=True),
        lax.all_gather(conv_bias, ("seq", "head"), axis=0, tiled=True),
        lax.all_gather(gate_gain, ("seq", "head"), axis=0, tiled=True),
        lax.all_gather(out_weight, ("seq", "head"), axis=0, tiled=True),
    )
    tok_dev = hidden_in.shape[1]
    head_devices = lax.axis_size("head")
    block_len = tok_dev * head_devices
    heads_here = HEADS // head_devices
    edge = CONV_K - 1
    inputs = hidden_in.astype(jnp.float32)
    gain_f = gain_all.astype(jnp.float32)
    normed_low = normed_rows(inputs, gain_f).astype(jnp.bfloat16)
    proj = jnp.einsum("mtd,dk->mtk", normed_low, in_all, preferred_element_type=jnp.float32)
    gate_in = proj[..., :D_INNER]
    conv_low = proj[..., D_INNER : D_INNER + CONV_CH].astype(jnp.bfloat16)
    step_low = proj[..., D_INNER + CONV_CH :].astype(jnp.bfloat16)
    rim = from_behind(conv_low[:, tok_dev - edge :, :], ("seq", "head"), 1)
    window = jnp.concatenate([rim, conv_low], axis=1).astype(jnp.float32)
    positions = lax.axis_index(("seq", "head")) * tok_dev - edge + jnp.arange(tok_dev + edge)
    seg_window = seg_ids(seq_starts, positions)
    valid = jnp.stack(
        [
            (seg_window[:, offset : offset + tok_dev] == seg_window[:, edge:]).astype(jnp.float32)
            for offset in range(CONV_K)
        ]
    )
    conv_w = conv_all.astype(jnp.float32)
    conv_b = bias_all.astype(jnp.float32)

    def convolve(window_in, taps, shifts):
        total = shifts[None, None, :]
        for offset in range(CONV_K):
            total = (
                total
                + taps[offset][None, None, :]
                * window_in[:, offset : offset + tok_dev, :]
                * valid[offset][..., None]
            )
        return jax.nn.silu(total)

    mixed_low = convolve(window, conv_w, conv_b).astype(jnp.bfloat16)
    keys_wide = jnp.tile(mixed_low[..., D_INNER:], (1, 1, head_devices))
    values_h, steps_h, keys_h = (
        lax.all_to_all(mixed_low[..., :D_INNER], "head", split_axis=2, concat_axis=1, tiled=True),
        lax.all_to_all(step_low, "head", split_axis=2, concat_axis=1, tiled=True),
        lax.all_to_all(keys_wide, "head", split_axis=2, concat_axis=1, tiled=True),
    )
    positions_h = lax.axis_index("seq") * block_len + jnp.arange(block_len)
    segs_h = seg_ids(seq_starts, positions_h)
    firsts_h = start_flags(seq_starts, positions_h)
    values_f = values_h.astype(jnp.float32).reshape(MICRO, block_len, heads_here, HEADDIM)
    keys_f = keys_h.astype(jnp.float32)
    steps_f = steps_h.astype(jnp.float32)

    def local_scan(bundle):
        return block_scan(
            bundle[0], bundle[1], bundle[2], decay_log, dt_bias, skip_gain, bundle[3], bundle[4]
        )

    partial_out, dev_decay, dev_state, reach = lax.map(
        local_scan, (values_f, keys_f, steps_f, segs_h, firsts_h)
    )
    decay_wide = dev_decay[:, :, None, None]
    state_in = carried_in(
        (decay_wide, dev_state),
        "seq",
        link_states,
        (jnp.ones_like(decay_wide), jnp.zeros_like(dev_state)),
    )[1]
    read_keys = keys_f[..., STATE:]
    mixer_h = partial_out + reach[..., None] * jnp.einsum(
        "mtk,mhpk->mthp", read_keys, state_in, precision=precise
    )
    mixer_low = mixer_h.reshape(MICRO, block_len, heads_here * HEADDIM).astype(jnp.bfloat16)
    mixer_tok = lax.all_to_all(mixer_low, "head", split_axis=1, concat_axis=2, tiled=True)
    mixer_f = mixer_tok.astype(jnp.float32)
    gate_f = gate_all.astype(jnp.float32)
    ynorm_low = gated_norm(mixer_f, gate_in, gate_f).astype(jnp.bfloat16)
    hidden_out = (
        inputs + jnp.einsum("mtk,kd->mtd", ynorm_low, out_all, preferred_element_type=jnp.float32)
    ).astype(jnp.bfloat16)
    grad_out_w = jnp.einsum("mtk,mtd->kd", ynorm_low, out_grad, preferred_element_type=jnp.float32)
    d_ynorm = jnp.einsum("mtd,kd->mtk", out_grad, out_all, preferred_element_type=jnp.float32)
    _, gate_pull = jax.vjp(gated_norm, mixer_f, gate_in, gate_f)
    d_mixer, d_gate_in, d_gate_gain = gate_pull(d_ynorm)
    d_mixer_h = lax.all_to_all(
        d_mixer.astype(jnp.bfloat16), "head", split_axis=2, concat_axis=1, tiled=True
    )
    d_mixer_f = d_mixer_h.astype(jnp.float32).reshape(MICRO, block_len, heads_here, HEADDIM)
    d_state_in = jnp.einsum("mth,mthp,mtk->mhpk", reach, d_mixer_f, read_keys, precision=precise)
    d_state_out = carried_in_2(
        (decay_wide, d_state_in),
        "seq",
        link_states,
        (jnp.ones_like(decay_wide), jnp.zeros_like(d_state_in)),
    )[1]
    d_decay = jnp.sum(d_state_out * state_in, axis=(2, 3))
    d_reach = jnp.einsum("mthp,mtk,mhpk->mth", d_mixer_f, read_keys, state_in, precision=precise)
    d_read_extra = jnp.einsum("mth,mthp,mhpk->mtk", reach, d_mixer_f, state_in, precision=precise)

    def local_back(bundle):
        values_one, keys_one, steps_one, segs_one, firsts_one, d_out, d_dec, d_state, d_rch = bundle

        def scan_part(values_in, keys_in, steps_in, log_in, bias_in, skip_in):
            return block_scan(
                values_in, keys_in, steps_in, log_in, bias_in, skip_in, segs_one, firsts_one
            )

        _, scan_pull = jax.vjp(
            scan_part, values_one, keys_one, steps_one, decay_log, dt_bias, skip_gain
        )
        return scan_pull((d_out, d_dec, d_state, d_rch))

    d_values, d_keys, d_steps, d_log, d_bias, d_skip = lax.map(
        local_back,
        (values_f, keys_f, steps_f, segs_h, firsts_h, d_mixer_f, d_decay, d_state_out, d_reach),
    )
    head_grads = lax.psum(
        (jnp.sum(d_log, axis=0), jnp.sum(d_bias, axis=0), jnp.sum(d_skip, axis=0)), "seq"
    )
    d_keys = d_keys + jnp.concatenate([jnp.zeros_like(d_read_extra), d_read_extra], axis=-1)
    d_values_low = d_values.reshape(MICRO, block_len, heads_here * HEADDIM).astype(jnp.bfloat16)
    d_values_tok, d_steps_tok = (
        lax.all_to_all(d_values_low, "head", split_axis=1, concat_axis=2, tiled=True),
        lax.all_to_all(
            d_steps.astype(jnp.bfloat16), "head", split_axis=1, concat_axis=2, tiled=True
        ),
    )
    d_keys_tok = lax.psum_scatter(d_keys, "head", scatter_dimension=1, tiled=True)
    d_keys_low = lax.optimization_barrier(d_keys_tok.astype(jnp.bfloat16)).astype(jnp.float32)
    d_mixed = jnp.concatenate([d_values_tok.astype(jnp.float32), d_keys_low], axis=-1)
    _, conv_pull = jax.vjp(convolve, window, conv_w, conv_b)
    d_window, d_conv_w, d_conv_b = conv_pull(d_mixed)
    rim_back = from_behind(d_window[:, :edge, :].astype(jnp.bfloat16), ("seq", "head"), -1).astype(
        jnp.float32
    )
    d_conv_in = d_window[:, edge:, :].at[:, tok_dev - edge :, :].add(rim_back)
    d_proj = jnp.concatenate(
        [d_gate_in, d_conv_in, d_steps_tok.astype(jnp.float32)], axis=-1
    ).astype(jnp.bfloat16)
    grad_in_w = jnp.einsum("mtd,mtk->dk", normed_low, d_proj, preferred_element_type=jnp.float32)
    d_normed = jnp.einsum("mtk,dk->mtd", d_proj, in_all, preferred_element_type=jnp.float32)
    _, norm_pull = jax.vjp(normed_rows, inputs, gain_f)
    d_inputs, d_norm_gain = norm_pull(d_normed)
    grad_in = (out_grad.astype(jnp.float32) + d_inputs).astype(jnp.bfloat16)
    g_norm, g_in, g_conv_w, g_conv_b, g_gate, g_out = (
        lax.psum_scatter(d_norm_gain, ("seq", "head"), scatter_dimension=0, tiled=True),
        lax.psum_scatter(grad_in_w, ("seq", "head"), scatter_dimension=0, tiled=True),
        lax.psum_scatter(d_conv_w, ("seq", "head"), scatter_dimension=1, tiled=True),
        lax.psum_scatter(d_conv_b, ("seq", "head"), scatter_dimension=0, tiled=True),
        lax.psum_scatter(d_gate_gain, ("seq", "head"), scatter_dimension=0, tiled=True),
        lax.psum_scatter(grad_out_w, ("seq", "head"), scatter_dimension=0, tiled=True),
    )
    return (
        hidden_out,
        grad_in,
        g_norm,
        g_in,
        g_conv_w,
        g_conv_b,
        head_grads[0],
        head_grads[1],
        head_grads[2],
        g_gate,
        g_out,
    )


def solution(mesh):
    placed = (
        P(None, ("seq", "head"), None),
        P(),
        P(("seq", "head")),
        P(("seq", "head"), None),
        P(None, ("seq", "head")),
        P(("seq", "head")),
        P("head"),
        P("head"),
        P("head"),
        P(("seq", "head")),
        P(("seq", "head"), None),
        P(None, ("seq", "head"), None),
    )
    return jax.shard_map(
        body,
        mesh=mesh,
        in_specs=placed,
        out_specs=(
            P(None, ("seq", "head"), None),
            P(None, ("seq", "head"), None),
            P(("seq", "head")),
            P(("seq", "head"), None),
            P(None, ("seq", "head")),
            P(("seq", "head")),
            P("head"),
            P("head"),
            P("head"),
            P(("seq", "head")),
            P(("seq", "head"), None),
        ),
        check_vma=False,
    )
```

profile of v0, /device:TPU:0, one launch (start us, length us, event | category | flops | bytes accessed | tf_op | source)
XLA Modules:
  0.0 2061.3 jit_solution(814401157519465881)
XLA Ops:
  9.7 44.1 %all-reduce.21 = (bf16[2048]{0:T(1024)(128)(2,1)S(1)}, bf16[4352]{0:T(1024)(128)(2,1)S(1)}) all-reduce(bf16[2048]{0:T(1024)(128)(2,1)S(1)} %dynamic-update-slice.4, bf16[4352]{0:T(1024)(128)(2,1)S(1)} %dynamic-update-slice.3), channel_id=1, replica_groups=mesh['seq'=4,'head'=8] {'seq','head'}, use_global_device_ids=true, to_apply=%add.14 | all-reduce | flops 6400 | bytes 25600
  53.8 41.9 %all-gather.4 = bf16[32,136,4]{1,2,0:T(4,128)(2,1)S(1)} all-gather(bf16[1,136,4]{1,2,0:T(4,128)(2,1)} %bitcast.655), channel_id=1, replica_groups=mesh['seq'=4,'head'=8] {'seq','head'}, dimensions={0}, use_global_device_ids=true | all-gather | bytes 35904 | tf_op jit(solution)/shard_map/all_gather | solution.py:153
  98.0 119.3 %all-gather.13.cloned.1.call-done = bf16[2048,8512]{1,0:T(8,128)(2,1)} async-done(((bf16[64,8512]{1,0:T(8,128)(2,1)}), bf16[2048,8512]{1,0:T(8,128)(2,1)}) %all-gather.13.cloned.1.call-update) | async-done | bytes 34865168 | tf_op jit(solution)/shard_map/all_gather | solution.py:152
  217.4 18.1 fusion.142
  262.5 9.8 all-to-all-done.1
  283.4 19.0 all-to-all-done
  317.5 53.1 %while.183 = (s32[]{:T(128)}, f32[2,512,8,64]{1,3,2,0:T(8,128)}, f32[2,8]{1,0:T(2,128)}, f32[2,8,64,128]{3,2,1,0:T(8,128)}, f32[2,512,8]{1,2,0:T(8,128)}, /*inde...) while((s32[]{:T(128)}, f32[2,512,8,64]{1,3,2,0:T(8,128)}, ...), condition=%wide.region_11.12_spmd.clone, body=%wide.region_4.11_spmd.sunk.clone | while | flops 1819731968 | bytes 31607216 | solution.py:213
  379.4 24.6 %all-gather.17.cloned.1.call-done = f32[8,8,64,128]{3,2,1,0:T(8,128)} async-done(((f32[2,8,64,128]{3,2,1,0:T(8,128)}), f32[8,8,64,128]{3,2,1,0:T(8,128)}) %all-gather.17.cloned.1.call-update) | async-done | bytes 2097168 | tf_op jit(solution)/shard_map/all_gather | solution.py:28
  418.3 70.2 %all-gather.6 = bf16[32,1,128]{2,1,0:T(2,128)(2,1)S(1)} all-gather(bf16[1,1,128]{2,1,0:T(2,128)(2,1)S(1)} %bitcast.657), channel_id=1, replica_groups=mesh['seq'=4,'head'=8] {'seq','head'}, dimensions={0}, use_global_device_ids=true | all-gather | bytes 8448 | tf_op jit(solution)/shard_map/all_gather | solution.py:155
  492.4 42.0 %all-gather.15.cloned.1.call-done = bf16[4096,2048]{1,0:T(8,128)(2,1)} async-done(((bf16[128,2048]{1,0:T(8,128)(2,1)}), bf16[4096,2048]{1,0:T(8,128)(2,1)}) %all-gather.15.cloned.1.call-update) | async-done | bytes 16777232 | tf_op jit(solution)/shard_map/all_gather | solution.py:156
  534.4 13.5 multiply_reduce_fusion.9
  561.3 30.8 %all_to_all.81 = bf16[8,2,32768]{2,1,0:T(2,128)(2,1)} all-to-all(bf16[8,2,32768]{2,1,0:T(2,128)(2,1)} %reshape.847), channel_id=1, replica_groups=mesh['seq'=4,'head'=8] {'head'}, dimensions={0} | all-to-all | bytes 2097152 | tf_op jit(solution)/shard_map/all_to_all | solution.py:239
  641.4 137.9 %while.187 = (s32[]{:T(128)}, bf16[2,512,8,64]{1,3,2,0:T(8,128)(2,1)}, f32[2,512,256]{2,1,0:T(8,128)}, bf16[2,512,8]{1,2,0:T(8,128)(2,1)}, f32[2,8]{1,0:T(2,128)...) while((s32[]{:T(128)}, ...), condition=%wide.region_41.42_spmd.clone, body=%wide.region_19.41_spmd.sunk.clone | while | flops 4657625088 | bytes 70709560 | solution.py:267
  670.5 9.0 while.186
  782.9 39.8 %all_to_all.82 = bf16[2,512,512]{2,0,1:T(2,128)(2,1)S(1)} all-to-all(bf16[2,512,512]{2,0,1:T(2,128)(2,1)S(1)} %copy.252), channel_id=1, replica_groups=mesh['seq'=4,'head'=8] {'head'}, dimensions={1} | all-to-all | bytes 2097152 | tf_op jit(solution)/shard_map/all_to_all | solution.py:277
  830.7 15.0 convolution_bitcast_fusion.3
  852.2 9.0 all_to_all.83
  865.4 25.9 %convolution_bitcast_fusion.2 = f32[2048,8512]{1,0:T(8,128)} fusion(bf16[2,64,64]{2,1,0:T(8,128)(2,1)S(1)} %copy.258, bf16[2,64,4352]{2,1,0:T(8,128)(2,1)S(1)} %scatter-add.4, bf16[2,64,4096]{2,1,0:T(8,128)(2,1)} %get-tuple-element.1617, bf16[2,64,2048]{2,1,0:T(8,128)(2,1)S(1)} %copy-done.11, f32[2048]{0:T(1024)S(1)} %copy-done.36, f32[2,64]{1,0:T(2,128)S(1)} %copy-done.59), kind=kOutput, calls=%fused_computation.179 | convolution fusion | flops 4470325248 | bytes 72442368 | tf_op jit(solution)/shard_map/mtd,mtk->dk/dot_general | solution.py:294
  901.9 9.9 all-reduce.20
  911.9 33.6 %all-reduce.24.cloned.1.call-done = f32[4,4352]{1,0:T(4,128)} async-done(((f32[4,4352]{1,0:T(4,128)}), f32[4,4352]{1,0:T(4,128)}) %all-reduce.24.cloned.1.call-update) | async-done | bytes 69648
  946.9 17.5 fusion.119
  964.4 44.9 %all-reduce.19 = (f32[2048]{0:T(1024)S(1)}, f32[4352]{0:T(1024)S(1)}, f32[4096]{0:T(1024)S(1)}) all-reduce(f32[2048]{0:T(1024)S(1)} %get-tuple-element.1431, f32[4352]{0:T(1024)S(1)} %get-tuple-element.1430, f32[4096]{0:T(1024)S(1)} %copy-done.70), channel_id=7, replica_groups=mesh['seq'=4,'head'=8] {'seq','head'}, use_global_device_ids=true, to_apply=%region_45.46.clone | all-reduce | flops 10496 | bytes 83968
  1012.3 300.5 %reduce-scatter.9.cloned.1.call-done = f32[128,2048]{1,0:T(8,128)} async-done(((f32[4096,2048]{1,0:T(8,128)}), f32[128,2048]{1,0:T(8,128)}) %reduce-scatter.9.cloned.1.call-update) | async-done | bytes 1048592 | tf_op jit(solution)/shard_map/reduce_scatter | solution.py:305
  1312.8 741.5 %reduce-scatter.7.cloned.1.call-done = f32[64,8512]{1,0:T(8,128)} async-done(((f32[2048,8512]{1,0:T(8,128)}), f32[64,8512]{1,0:T(8,128)}) %reduce-scatter.7.cloned.1.call-update) | async-done | bytes 2179088 | tf_op jit(solution)/shard_map/reduce_scatter | solution.py:301
  (749 shorter events, 396.4 us)
Async XLA Ops:
  7.2 210.2 %copy-start.10 = (bf16[2,64,2048]{2,1,0:T(8,128)(2,1)S(1)}, bf16[2,64,2048]{2,1,0:T(8,128)(2,1)}, u32[]{:S(2)}) copy-start(bf16[2,64,2048]{2,1,0:T(8,128)(2,1)} %param.28) | copy-start | bytes 1572868
  7.2 210.2 %all-gather.13.cloned.1.call-start = ((), (), s32[]{:S(2)}) async-start(), calls=%async_computation.10 | async-start | bytes 36225024 | tf_op jit(solution)/shard_map/all_gather | solution.py:152
  53.8 181.6 %copy-start.35 = (f32[2048]{0:T(1024)}, f32[2048]{0:T(1024)S(1)}, u32[]{:S(2)}) copy-start(f32[2048]{0:T(1024)S(1)} %convert_element_type.185) | copy-start | bytes 24580
  97.9 137.5 %copy-start.81 = (f32[2,64]{1,0:T(2,128)}, f32[2,64]{1,0:T(2,128)S(1)}, u32[]{:S(2)}) copy-start(f32[2,64]{1,0:T(2,128)S(1)} %fusion.122) | copy-start | bytes 1540
  97.9 137.5 %copy-start.58 = (f32[2,64]{1,0:T(2,128)}, f32[2,64]{1,0:T(2,128)S(1)}, u32[]{:S(2)}) copy-start(f32[2,64]{1,0:T(2,128)S(1)} %fusion.131) | copy-start | bytes 1540
  98.0 148.8 %copy-start.73 = (f32[2,64]{1,0:T(2,128)}, f32[2,64]{1,0:T(2,128)S(1)}, u32[]{:S(2)}) copy-start(f32[2,64]{1,0:T(2,128)S(1)} %get-tuple-element.1623) | copy-start | bytes 1540
  98.0 148.8 %copy-start.75 = (f32[2,64]{1,0:T(2,128)}, f32[2,64]{1,0:T(2,128)S(1)}, u32[]{:S(2)}) copy-start(f32[2,64]{1,0:T(2,128)S(1)} %get-tuple-element.1624) | copy-start | bytes 1540
  98.0 148.8 %copy-start.77 = (f32[2,64]{1,0:T(2,128)}, f32[2,64]{1,0:T(2,128)S(1)}, u32[]{:S(2)}) copy-start(f32[2,64]{1,0:T(2,128)S(1)} %get-tuple-element.1625) | copy-start | bytes 1540
  235.5 9.7 collective-permute-start
  239.8 12.0 all-to-all-start.2
  251.7 20.6 all-to-all-start.1
  272.3 30.1 %all-to-all-start = ((bf16[8,2,32768]{2,1,0:T(2,128)(2,1)}), bf16[8,2,32768]{2,1,0:T(2,128)(2,1)S(1)}, u32[]{:S(2)}, u32[]{:S(2)}) async-start(bf16[8,2,32768]{2,1,0:T(2,128)(2,1)} %reshape.841), calls=%async_computation | async-start | bytes 2097152 | tf_op jit(solution)/shard_map/all_to_all | solution.py:197
  275.9 128.2 %all-gather.17.cloned.1.call-start = ((), (), s32[]{:S(2)}) async-start(), calls=%async_computation.15 | async-start | bytes 2621440 | tf_op jit(solution)/shard_map/all_gather | solution.py:28
  370.6 163.8 %all-gather.15.cloned.1.call-start = ((), (), s32[]{:S(2)}) async-start(), calls=%async_computation.11 | async-start | bytes 17301504 | tf_op jit(solution)/shard_map/all_gather | solution.py:156
  413.7 74.9 %all-to-all-start.3 = ((bf16[2,512,512]{2,0,1:T(2,128)(2,1)}), bf16[2,512,512]{2,0,1:T(2,128)(2,1)S(1)}, u32[]{:S(2)}, u32[]{:S(2)}) async-start(bf16[2,512,512]{2,0,1:T(2,128)(2,1)} %copy.244), calls=%async_computation.3 | async-start | bytes 2097152 | tf_op jit(solution)/shard_map/all_to_all | solution.py:228
  418.3 213.3 %all-gather.19.cloned.1.call-start = ((), (), s32[]{:S(2)}) async-start(), calls=%async_computation.16 | async-start | bytes 1310720 | tf_op jit(solution)/shard_map/all_gather | solution.py:46
  488.6 59.3 %copy-start.37 = (f32[32,1,128]{2,1,0:T(1,128)}, f32[32,1,128]{2,1,0:T(1,128)S(1)}, u32[]{:S(2)}) copy-start(f32[32,1,128]{2,1,0:T(1,128)S(1)} %convert_element_type.242) | copy-start | bytes 49156
  492.4 55.5 %copy-start.65 = (f32[2,64]{1,0:T(2,128)}, f32[2,64]{1,0:T(2,128)S(1)}, u32[]{:S(2)}) copy-start(f32[2,64]{1,0:T(2,128)S(1)} %fusion.132) | copy-start | bytes 1540
  606.9 217.1 %reduce-scatter.5.cloned.1.call-start = ((), (), s32[]{:S(2)}) async-start(), calls=%async_computation.12 | async-start | bytes 1179648 | tf_op jit(solution)/shard_map/reduce_scatter | solution.py:282
  781.9 163.6 %all-reduce.24.cloned.1.call-start = ((), (), s32[]{:S(2)}) async-start(), calls=%async_computation.17 | async-start | bytes 139264
  830.7 482.1 %reduce-scatter.9.cloned.1.call-start = ((), (), s32[]{:S(2)}) async-start(), calls=%async_computation.14 | async-start | bytes 34603008 | tf_op jit(solution)/shard_map/reduce_scatter | solution.py:305
  845.7 1208.6 %reduce-scatter.7.cloned.1.call-start = ((), (), s32[]{:S(2)}) async-start(), calls=%async_computation.13 | async-start | bytes 72450048 | tf_op jit(solution)/shard_map/reduce_scatter | solution.py:301
  850.4 13.4 collective-permute-start.1
  946.9 64.2 %copy-start.82 = (f32[2,64]{1,0:T(2,128)S(1)}, f32[2,64]{1,0:T(2,128)}, u32[]{:S(2)}) copy-start(f32[2,64]{1,0:T(2,128)} %copy-done.81) | copy-start | bytes 1540
  (135 other events, 801.8 us)
Sparse Core Ops, SparseCore 0:
  10.9 206.4 all-gather.12
  370.7 33.2 all-gather.16
  407.0 127.3 all-gather.14
  607.0 24.5 all-gather.18
  782.0 35.7 reduce-scatter.4
  830.8 114.6 all-reduce.23
  948.4 364.3 reduce-scatter.8
  1315.7 738.5 reduce-scatter.6
where the time goes:
time: 2070 us; the launch traced here: 2060 us
  waiting for transfers between devices  1300 us (63%)
  blocking collectives  307 us (15%)
  matrix products  185 us (9%)
  local copies, waits for them, and re-layouts  129 us (6%)
  other arithmetic  104 us (5%)
  starting transfers between devices  23.1 us (1%)
    reduce_scatter x1, waiting for transfers between devices, body(): lax.psum_scatter(grad_in_w, ('seq', 'head'), scatter_dimension=0, tiled=T...  742 us
    reduce_scatter x1, waiting for transfers between devices, body(): lax.psum_scatter(grad_out_w, ('seq', 'head'), scatter_dimension=0, tiled=...  301 us
    all_gather x1, waiting for transfers between devices, body(): lax.all_gather(in_weight, ('seq', 'head'), axis=0, tiled=True)  119 us
    unnamed x2, blocking collectives  89 us
    all_gather x1, blocking collectives, body(): lax.all_gather(gate_gain, ('seq', 'head'), axis=0, tiled=True)  70.2 us
    all_gather x1, waiting for transfers between devices, body(): lax.all_gather(out_weight, ('seq', 'head'), axis=0, tiled=True)  42 us
    all_gather x1, blocking collectives, body(): lax.all_gather(conv_weight, ('seq', 'head'), axis=1, tiled=True)  41.9 us
  transfers between devices with their start and end apart: 14, of which 9 were waited for; matrix products, arithmetic and copies ran while one was open for 6% of the time, Pallas kernels for 0%

commit v1 on v0

v1 whole, which is shorter than its diff:
```python
import jax
import jax.numpy as jnp
from jax import lax
from jax.sharding import PartitionSpec as P

HEADS = 64
HEADDIM = 64
STATE = 128
CONV_K = 4
SCAN_BLOCK = 256
D_INNER = 4096
CONV_CH = 4352
EDGE = CONV_K - 1
EPS = 1e-05

f32 = jnp.float32
bf16 = jnp.bfloat16
BOTH = ("seq", "head")


def dot(spec, a, b):
    return jnp.einsum(spec, a, b, preferred_element_type=f32)


def halves(v):
    high = lax.reduce_precision(v, 8, 7)
    return high.astype(bf16), (v - high).astype(bf16)


def halved(spec, a, b):
    return dot(spec, a, b[0]) + dot(spec, a, b[1])


def three_parts(v):
    parts = []
    for _ in range(3):
        part = lax.reduce_precision(v, 8, 7)
        parts.append(part.astype(bf16))
        v = v - part
    return parts


def linked(payload, back):
    count = lax.axis_size("seq")
    total, reach = 0.0, 1.0
    for k in range(1, count):
        if back:
            pairs = [(i, i - k) for i in range(k, count)]
        else:
            pairs = [(i, i + k) for i in range(count - k)]
        got = lax.ppermute(payload, "seq", pairs).astype(f32)
        total = total + reach * got[:, :, :STATE]
        reach = reach * got[:, :, STATE : STATE + 1]
    return total


def silu_parts(v):
    sig = jax.nn.sigmoid(v)
    return v * sig, sig * (1.0 + v * (1.0 - sig))


def body(
    hidden_in,
    seq_starts,
    norm_gain,
    in_weight,
    conv_weight,
    conv_bias,
    decay_log,
    dt_bias,
    skip_gain,
    gate_gain,
    out_weight,
    out_grad,
):
    seqs, heads = lax.axis_size("seq"), lax.axis_size("head")
    s_i, h_i = lax.axis_index("seq"), lax.axis_index("head")
    micro, tok, width = hidden_in.shape
    rows = in_weight.shape[0]
    shard = tok * heads
    runs = seqs if HEADS % (seqs * heads) == 0 else 1
    run_ch = D_INNER // (runs * heads)
    run_heads = HEADS // (runs * heads)
    chans, n_heads = runs * run_ch, runs * run_heads
    key_ch = 2 * STATE // heads
    conv_share, gate_share, head_share = conv_bias.shape[0], gate_gain.shape[0], decay_log.shape[0]

    def mine(x, size):
        lead = x.shape[:-1]
        x = x.reshape(lead + (runs, heads, size))
        x = lax.dynamic_index_in_dim(x, h_i, len(lead) + 1, False)
        return x.reshape(lead + (runs * size,))

    def columns(x, size):
        x = x.reshape(rows, runs, heads, size)
        return jnp.transpose(x, (2, 0, 1, 3)).reshape(heads, rows, runs * size)

    extras = jnp.concatenate(
        [norm_gain, conv_weight.reshape(-1), conv_bias, gate_gain]
        + three_parts(decay_log)
        + three_parts(dt_bias)
        + three_parts(skip_gain)
    )
    extra_cols = -(-extras.shape[0] // rows)
    extras = jnp.pad(extras, (0, extra_cols * rows - extras.shape[0])).reshape(extra_cols, rows)
    key_p = jnp.transpose(
        in_weight[:, 2 * D_INNER : 2 * D_INNER + 2 * STATE].reshape(rows, heads, key_ch), (1, 2, 0)
    )
    step_p = jnp.transpose(
        in_weight[:, 2 * D_INNER + 2 * STATE :].reshape(rows, runs, heads, run_heads), (2, 1, 3, 0)
    ).reshape(heads, n_heads, rows)
    small_p = jnp.concatenate(
        [key_p, step_p, jnp.broadcast_to(extras[None], (heads,) + extras.shape)], axis=1
    )

    def spread(x):
        x = lax.all_to_all(x, "head", split_axis=0, concat_axis=0, tiled=True)
        return lax.all_gather(x, "seq", axis=0, tiled=False)

    w_val = spread(columns(in_weight[:, D_INNER : 2 * D_INNER], run_ch)).reshape(width, chans)
    small = spread(small_p)
    w_gate = spread(columns(in_weight[:, :D_INNER], run_ch)).reshape(width, chans)
    n_small = key_ch + n_heads
    w_small = jnp.transpose(small[:, :, :n_small], (2, 0, 1, 3)).reshape(n_small, width)
    extras = small[:, :, n_small:].reshape(seqs * heads, -1)
    at = 0

    def take(size):
        nonlocal at
        at += size
        return extras[:, at - size : at]

    gain = take(rows).reshape(width).astype(f32)
    conv_w = jnp.transpose(take(CONV_K * conv_share).reshape(-1, CONV_K, conv_share), (1, 0, 2))
    conv_w = conv_w.reshape(CONV_K, CONV_CH).astype(f32)
    conv_b = take(conv_share).reshape(1, CONV_CH).astype(f32)
    conv_p = jnp.concatenate([conv_w, conv_b], axis=0)
    gate_g = mine(take(gate_share).reshape(D_INNER), run_ch).astype(f32)

    def head_param():
        x = take(3 * head_share)[:heads].reshape(heads, 3, head_share).astype(f32)
        return mine((x[:, 0] + x[:, 1] + x[:, 2]).reshape(HEADS), run_heads)

    decay_mine, bias_mine, skip_mine = head_param(), head_param(), head_param()
    conv_val = mine(conv_p[:, :D_INNER], run_ch)
    conv_key = lax.dynamic_slice_in_dim(conv_p[:, D_INNER:], h_i * key_ch, key_ch, 1)
    if runs == seqs:
        w_out = lax.all_gather(out_weight, "seq", axis=0, tiled=True)
    else:
        w_out = lax.all_gather(out_weight, BOTH, axis=0, tiled=True)
        w_out = lax.dynamic_slice_in_dim(w_out, h_i * chans, chans, 0)

    inputs = lax.all_gather(hidden_in, "head", axis=1, tiled=True).astype(f32)
    grad_rows = lax.all_gather(out_grad, "head", axis=1, tiled=True)
    inv = lax.rsqrt(jnp.mean(inputs * inputs, axis=-1, keepdims=True) + EPS)
    unit = inputs * inv
    normed_low = (unit * gain).astype(bf16)
    val_in = dot("mtd,dk->mtk", normed_low, w_val).astype(bf16)
    small_in = dot("kd,mtd->mkt", w_small, normed_low).astype(bf16)
    key_in, step_low = small_in[:, :key_ch], small_in[:, key_ch:].astype(f32)
    gate_in = dot("mtd,dk->mtk", normed_low, w_gate)

    positions = s_i * shard - EDGE + jnp.arange(shard + EDGE)
    segs = jnp.sum((seq_starts[:, None, :] <= positions[None, :, None]).astype(jnp.int32), axis=2)
    firsts = jnp.sum(
        (seq_starts[:, None, :] == positions[None, EDGE:, None]).astype(f32), axis=2
    )
    valid = [
        (segs[:, k : k + shard] == segs[:, EDGE:]).astype(f32) for k in range(CONV_K)
    ]
    segs = segs[:, EDGE:]
    rim = jnp.concatenate(
        [val_in[:, shard - EDGE :], jnp.swapaxes(key_in[:, :, shard - EDGE :], 1, 2)], axis=2
    )
    forward = [(i, i + 1) for i in range(seqs - 1)]
    rim = lax.ppermute(rim, "seq", forward)
    val_win = jnp.concatenate([rim[:, :, :chans], val_in], axis=1).astype(f32)
    key_win = jnp.concatenate(
        [jnp.swapaxes(rim[:, :, chans:], 1, 2), key_in], axis=2
    ).astype(f32)
    val_tot = conv_val[CONV_K]
    key_tot = conv_key[CONV_K][:, None]
    for k in range(CONV_K):
        val_tot = val_tot + conv_val[k] * val_win[:, k : k + shard] * valid[k][:, :, None]
        key_tot = key_tot + conv_key[k][:, None] * key_win[:, :, k : k + shard] * valid[k][:, None]
    vals = jax.nn.silu(val_tot).astype(bf16)
    keys = jax.nn.silu(key_tot).astype(bf16)
    keys = lax.all_gather(keys, "head", axis=1, tiled=True)

    blocks = shard // SCAN_BLOCK
    rate = -jnp.exp(decay_mine)
    pre_step = step_low + bias_mine[:, None]
    step = jax.nn.softplus(pre_step)
    logs = jnp.cumsum((step * rate[:, None]).reshape(micro, n_heads, blocks, SCAN_BLOCK), axis=-1)
    step_b = step.reshape(micro, n_heads, blocks, SCAN_BLOCK)
    seg_b = segs.reshape(micro, blocks, SCAN_BLOCK)
    first_b = firsts.reshape(micro, blocks, SCAN_BLOCK)
    vals_b = vals.reshape(micro, blocks, SCAN_BLOCK, n_heads, HEADDIM).astype(f32)
    wkey = keys[:, :STATE].reshape(micro, STATE, blocks, SCAN_BLOCK)
    rkey = keys[:, STATE:].reshape(micro, STATE, blocks, SCAN_BLOCK)
    causal = jnp.arange(SCAN_BLOCK)[:, None] >= jnp.arange(SCAN_BLOCK)[None, :]
    same = (seg_b[..., :, None] == seg_b[..., None, :]) & causal
    open_seq = (jnp.cumsum(first_b, axis=-1) == 0)[:, None]
    carry = jnp.where(open_seq, jnp.exp(logs), 0.0)
    tail = (seg_b == seg_b[..., -1:])[:, None]
    to_end = jnp.where(tail, jnp.exp(jnp.where(tail, logs[..., -1:] - logs, 0.0)), 0.0)
    stepped = jnp.einsum("mjcq,mcqjp->mcqjp", step_b, vals_b)
    ending = jnp.einsum("mjcq,mcqjp->mcqjp", to_end, stepped).astype(bf16)
    stepped = stepped.astype(bf16)
    block_state = dot("mncq,mcqjp->mcjnp", wkey, ending)
    block_decay = carry[..., -1]
    state = jnp.zeros_like(block_state[:, 0])
    reach = jnp.ones_like(block_decay[:, :, 0])
    before, prefix = [], []
    for c in range(blocks):
        before.append(state)
        prefix.append(reach)
        state = block_decay[:, :, c, None, None] * state + block_state[:, c]
        reach = block_decay[:, :, c] * reach
    decay_row = jnp.broadcast_to(reach[:, :, None, None], (micro, n_heads, 8, HEADDIM))
    state_in = linked(jnp.concatenate([state, decay_row], axis=2).astype(bf16), False)
    starts = jnp.stack(
        [before[c] + prefix[c][:, :, None, None] * state_in for c in range(blocks)], axis=1
    )
    starts_low = halves(starts)
    scores = jnp.where(same, dot("mncq,mncs->mcqs", rkey, wkey), 0.0)
    spread_log = logs[..., :, None] - logs[..., None, :]
    within = jnp.exp(jnp.minimum(spread_log, 0.0))
    weights = (scores[:, None] * within).astype(bf16)
    inner = dot("mjcqs,mcsjp->mcqjp", weights, stepped)
    carried = jnp.einsum("mjcq,mcqjp->mcqjp", carry, halved("mncq,mcjnp->mcqjp", rkey, starts_low))
    mixer = inner + carried + skip_mine[:, None] * vals_b
    mixer = mixer.astype(bf16).astype(f32).reshape(micro, shard, chans)

    gate_act, gate_slope = silu_parts(gate_in)
    gated = mixer * gate_act
    d_ynorm = dot("mtd,kd->mtk", grad_rows, w_out)
    pulled = d_ynorm * gate_g
    sums = jnp.stack([jnp.sum(gated * gated, axis=-1), jnp.sum(gated * pulled, axis=-1)])
    sums = lax.psum(sums, "head")
    scale = lax.rsqrt(sums[0] / D_INNER + EPS)[..., None]
    ynorm_low = (gated * scale * gate_g).astype(bf16)
    out_part = dot("mtk,kd->mtd", ynorm_low, w_out).astype(bf16)
    out_sum = lax.psum_scatter(out_part, "head", scatter_dimension=1, tiled=True)
    hidden_out = (hidden_in.astype(f32) + out_sum.astype(f32)).astype(bf16)
    grad_out_part = dot("mtk,mtd->kd", ynorm_low, grad_rows).astype(bf16)
    grad_gate_gain = jnp.sum(d_ynorm * gated * scale, axis=(0, 1))
    d_gated = scale * (pulled - gated * (scale * scale * sums[1][..., None] / D_INNER))
    d_mix = (d_gated * gate_act).astype(bf16)
    d_gate = (d_gated * mixer * gate_slope).astype(bf16)

    d_mix_f = d_mix.astype(f32).reshape(micro, blocks, SCAN_BLOCK, n_heads, HEADDIM)
    d_mix_b = d_mix.reshape(micro, blocks, SCAN_BLOCK, n_heads, HEADDIM)
    carry_d = jnp.einsum("mjcq,mcqjp->mcqjp", carry, d_mix_f).astype(bf16)
    block_adj = dot("mncq,mcqjp->mcjnp", rkey, carry_d)
    adj = jnp.zeros_like(block_adj[:, 0])
    for c in reversed(range(blocks)):
        adj = block_decay[:, :, c, None, None] * adj + block_adj[:, c]
    adj_out = linked(jnp.concatenate([adj, decay_row], axis=2).astype(bf16), True)
    ends = [None] * blocks
    for c in reversed(range(blocks)):
        ends[c] = adj_out
        adj_out = block_decay[:, :, c, None, None] * adj_out + block_adj[:, c]
    ends = jnp.stack(ends, axis=1)
    ends_low = ends.astype(bf16)
    d_weights = dot("mcqjp,mcsjp->mjcqs", d_mix_b, stepped) * within
    d_scores = jnp.where(same, jnp.sum(d_weights, axis=1), 0.0).astype(bf16)
    pairs = d_weights * scores[:, None]
    d_logs = jnp.sum(pairs, axis=-1) - jnp.sum(pairs, axis=-2)
    back_state = dot("mncq,mcjnp->mcqjp", wkey, ends_low)
    d_stepped = dot("mjcqs,mcqjp->mcsjp", weights, d_mix_b)
    d_stepped = d_stepped + jnp.einsum("mjcq,mcqjp->mcqjp", to_end, back_state)
    from_end = jnp.einsum("mcqjp,mcqjp->mjcq", ending.astype(f32), back_state)
    d_logs = d_logs + jnp.einsum("mcqjp,mcqjp->mjcq", d_mix_f, carried) - from_end
    d_last = jnp.sum(from_end, axis=-1)
    d_last = d_last + block_decay * jnp.einsum("mcjnp,mcjnp->mjc", ends, starts)
    d_logs = d_logs.at[..., -1].add(d_last)
    d_decay = jnp.flip(jnp.cumsum(jnp.flip(d_logs, -1), axis=-1), -1)
    d_decay = (d_decay * (1.0 - first_b)[:, None]).reshape(micro, n_heads, shard)
    d_step = jnp.einsum("mcqjp,mcqjp->mjcq", vals_b, d_stepped).reshape(micro, n_heads, shard)
    d_step = d_step + d_decay * rate[:, None]
    grad_decay = jnp.sum(d_decay * step * rate[:, None], axis=(0, 2))
    grad_skip = jnp.einsum("mcqjp,mcqjp->j", d_mix_f, vals_b)
    d_step_raw = d_step * jax.nn.sigmoid(pre_step)
    grad_bias = jnp.sum(d_step_raw, axis=(0, 2))
    d_vals = jnp.einsum("mjcq,mcqjp->mcqjp", step_b, d_stepped) + skip_mine[:, None] * d_mix_f
    d_vals = d_vals.astype(bf16).astype(f32).reshape(micro, shard, chans)
    d_write = dot("mcqs,mncq->mncs", d_scores, rkey) + dot("mcqjp,mcjnp->mncq", ending, ends_low)
    d_read = dot("mcqs,mncs->mncq", d_scores, wkey) + halved("mcqjp,mcjnp->mncq", carry_d, starts_low)
    d_keys = jnp.concatenate([d_write, d_read], axis=1).reshape(micro, 2 * STATE, shard)
    d_keys = lax.psum_scatter(d_keys, "head", scatter_dimension=1, tiled=True)
    d_keys = lax.reduce_precision(d_keys, 8, 7)

    d_val_tot = d_vals * silu_parts(val_tot)[1]
    d_key_tot = d_keys * silu_parts(key_tot)[1]
    d_val_win, d_key_win = 0.0, 0.0
    grad_conv_val, grad_conv_key = [], []
    for k in range(CONV_K):
        held = d_val_tot * valid[k][:, :, None]
        grad_conv_val.append(jnp.sum(held * val_win[:, k : k + shard], axis=(0, 1)))
        d_val_win = d_val_win + jnp.pad(held * conv_val[k], ((0, 0), (k, EDGE - k), (0, 0)))
        held = d_key_tot * valid[k][:, None]
        grad_conv_key.append(jnp.sum(held * key_win[:, :, k : k + shard], axis=(0, 2)))
        d_key_win = d_key_win + jnp.pad(
            held * conv_key[k][:, None], ((0, 0), (0, 0), (k, EDGE - k))
        )
    grad_conv_val.append(jnp.sum(d_val_tot, axis=(0, 1)))
    grad_conv_key.append(jnp.sum(d_key_tot, axis=(0, 2)))
    rim_back = jnp.concatenate(
        [d_val_win[:, :EDGE], jnp.swapaxes(d_key_win[:, :, :EDGE], 1, 2)], axis=2
    )
    rim_back = lax.ppermute(rim_back, "seq", [(i + 1, i) for i in range(seqs - 1)])
    d_val_in = d_val_win[:, EDGE:].at[:, shard - EDGE :].add(rim_back[:, :, :chans])
    d_key_in = d_key_win[:, :, EDGE:].at[:, :, shard - EDGE :].add(
        jnp.swapaxes(rim_back[:, :, chans:], 1, 2)
    )
    d_val_in = d_val_in.astype(bf16)
    d_small = jnp.concatenate([d_key_in, d_step_raw], axis=1).astype(bf16)

    grad_w_gate = dot("mtd,mtk->dk", normed_low, d_gate).astype(bf16)
    grad_w_val = dot("mtd,mtk->dk", normed_low, d_val_in).astype(bf16)
    grad_w_small = dot("mtd,mkt->dk", normed_low, d_small).astype(bf16)
    d_normed = (
        dot("mtk,dk->mtd", d_gate, w_gate)
        + dot("mtk,dk->mtd", d_val_in, w_val)
        + dot("mkt,kd->mtd", d_small, w_small)
    )
    grad_norm_part = jnp.sum(d_normed * unit, axis=(0, 1))
    d_normed = lax.psum_scatter(
        d_normed.astype(bf16), "head", scatter_dimension=1, tiled=True
    ).astype(f32)
    own = hidden_in.astype(f32)
    own_inv = lax.rsqrt(jnp.mean(own * own, axis=-1, keepdims=True) + EPS)
    d_unit = d_normed * gain
    d_inputs = own_inv * (
        d_unit - own * (own_inv * own_inv * jnp.mean(d_unit * own, axis=-1, keepdims=True))
    )
    grad_in = (out_grad.astype(f32) + d_inputs).astype(bf16)

    def collect(part):
        part = lax.psum_scatter(part, "seq", scatter_dimension=0, tiled=True)
        return lax.all_to_all(
            part.reshape(heads, rows, -1), "head", split_axis=0, concat_axis=0, tiled=True
        ).astype(f32)

    def uncolumns(x, size):
        x = x.reshape(heads, rows, runs, size)
        return jnp.transpose(x, (1, 2, 0, 3)).reshape(rows, runs * heads * size)

    g_gate, g_val, g_small = collect(grad_w_gate), collect(grad_w_val), collect(grad_w_small)
    grad_in_weight = jnp.concatenate(
        [
            uncolumns(g_gate, run_ch),
            uncolumns(g_val, run_ch),
            jnp.transpose(g_small[:, :, :key_ch], (1, 0, 2)).reshape(rows, -1),
            uncolumns(g_small[:, :, key_ch:], run_heads),
        ],
        axis=1,
    )
    if runs == seqs:
        grad_out_weight = lax.psum_scatter(
            grad_out_part, "seq", scatter_dimension=0, tiled=True
        ).astype(f32)
    else:
        full = jnp.zeros((D_INNER, width), bf16)
        full = lax.dynamic_update_slice_in_dim(full, grad_out_part, h_i * chans, 0)
        grad_out_weight = lax.psum_scatter(full, BOTH, scatter_dimension=0, tiled=True).astype(f32)

    def placed(x, size):
        lead = x.shape[:-1]
        full = jnp.zeros(lead + (runs, heads, size), f32)
        full = lax.dynamic_update_index_in_dim(
            full, x.reshape(lead + (runs, size)), h_i, len(lead) + 1
        )
        return full.reshape(lead + (runs * heads * size,))

    conv_val_g = placed(jnp.stack(grad_conv_val), run_ch)
    conv_key_g = lax.dynamic_update_slice_in_dim(
        jnp.zeros((CONV_K + 1, 2 * STATE), f32), jnp.stack(grad_conv_key), h_i * key_ch, 1
    )
    conv_g = jnp.concatenate([conv_val_g, conv_key_g], axis=1)
    head_g = placed(jnp.stack([grad_decay, grad_bias, grad_skip]), run_heads)
    gate_g_full = placed(grad_gate_gain, run_ch)
    conv_g, head_g, gate_g_full, norm_g = lax.psum(
        (conv_g, head_g, gate_g_full, grad_norm_part), BOTH
    )
    place = s_i * heads + h_i
    conv_g = lax.dynamic_slice_in_dim(conv_g, place * conv_share, conv_share, 1)
    head_g = lax.dynamic_slice_in_dim(head_g, h_i * head_share, head_share, 1)
    return (
        hidden_out,
        grad_in,
        lax.dynamic_slice_in_dim(norm_g, place * rows, rows, 0),
        grad_in_weight,
        conv_g[:CONV_K],
        conv_g[CONV_K],
        head_g[0],
        head_g[1],
        head_g[2],
        lax.dynamic_slice_in_dim(gate_g_full, place * gate_share, gate_share, 0),
        grad_out_weight,
    )


def solution(mesh):
    tokens = P(None, BOTH, None)
    by_rows = P(BOTH, None)
    return jax.shard_map(
        body,
        mesh=mesh,
        in_specs=(
            tokens,
            P(),
            P(BOTH),
            by_rows,
            P(None, BOTH),
            P(BOTH),
            P("head"),
            P("head"),
            P("head"),
            P(BOTH),
            by_rows,
            tokens,
        ),
        out_specs=(
            tokens,
            tokens,
            P(BOTH),
            by_rows,
            P(None, BOTH),
            P(BOTH),
            P("head"),
            P("head"),
            P("head"),
            P(BOTH),
            by_rows,
        ),
        check_vma=False,
    )
```

time: 2070 us -> 759 us (0.37)
  waiting for transfers between devices: 1300 us -> 330 us
  blocking collectives: 307 us -> 155 us
  matrix products: 185 us -> 86.9 us
  local copies, waits for them, and re-layouts: 129 us -> 64.6 us
  other arithmetic: 104 us -> 66.5 us
    reduce_scatter x3 -> x7, waiting for transfers between devices: 1040 us -> 155 us  [the longest x1 49.2 us: body(): lax.psum_scatter(out_part, 'head', scatter_dimension=1, tiled=True)]
    all_gather x4 -> x5, waiting for transfers between devices: 189 us -> 37.9 us  [the longest x2 36.4 us: spread(): return lax.all_gather(x, 'seq', axis=0, tiled=False)]
    dot_general x40 -> x23, matrix products: 185 us -> 82.9 us  [dot(): return jnp.einsum(spec, a, b, preferred_element_type=f32)]
    all_gather x4 -> x2, blocking collectives: 128 us -> 28.4 us  [the longest x1 14.7 us: body(): keys = lax.all_gather(keys, 'head', axis=1, tiled=True)]
    unnamed x2 -> x0, blocking collectives: 89 us -> none
    psum x0 -> x1, waiting for transfers between devices: none -> 81.6 us  [body(): lax.psum((conv_g, head_g, gate_g_full, grad_norm_part), BOTH)]
    psum x1 -> x2, blocking collectives: 9.93 us -> 56.1 us  [the longest x1 40.7 us: body(): lax.psum((conv_g, head_g, gate_g_full, grad_norm_part), BOTH)]
    ppermute x2 -> x8, waiting for transfers between devices: 0.01 us -> 38.9 us  [the longest x6 34.9 us: linked(): got = lax.ppermute(payload, 'seq', pairs).astype(f32)]
  transfers between devices with their start and end apart: 14 -> 24, of which waited for: 9 -> 14; matrix products, arithmetic and copies ran while one was open for 6% -> 21% of each run, Pallas kernels for 0% -> 0%
where the time goes in v1:
time: 759 us; the launch traced here: 751 us
  waiting for transfers between devices  330 us (43%)
  blocking collectives  155 us (20%)
  matrix products  86.9 us (11%)
  other arithmetic  66.5 us (9%)
  local copies, waits for them, and re-layouts  64.6 us (9%)
  starting transfers between devices  30.8 us (4%)
  between operations  16.2 us (2%)
    dot_general x23, matrix products, dot(): return jnp.einsum(spec, a, b, preferred_element_type=f32)  82.9 us
    psum x1, waiting for transfers between devices, body(): lax.psum((conv_g, head_g, gate_g_full, grad_norm_part), BOTH)  81.6 us
    all_to_all x2, blocking collectives, spread(): x = lax.all_to_all(x, 'head', split_axis=0, concat_axis=0, tiled=True)  62.8 us
    reduce_scatter x1, waiting for transfers between devices, body(): lax.psum_scatter(out_part, 'head', scatter_dimension=1, tiled=True)  49.2 us
    reduce_scatter x1, waiting for transfers between devices, body(): lax.psum_scatter(d_normed.astype(bf16), 'head', scatter_dimension=1, tile...  45.5 us
    psum x1, blocking collectives, body(): lax.psum((conv_g, head_g, gate_g_full, grad_norm_part), BOTH)  40.7 us
    reduce_scatter x1, waiting for transfers between devices, body(): lax.psum_scatter(grad_out_part, 'seq', scatter_dimension=0, tiled=True)  37.4 us
    all_gather x2, waiting for transfers between devices, spread(): return lax.all_gather(x, 'seq', axis=0, tiled=False)  36.4 us
  transfers between devices with their start and end apart: 24, of which 14 were waited for; matrix products, arithmetic and copies ran while one was open for 21% of the time, Pallas kernels for 0%

profile of v1, /device:TPU:0, one launch (start us, length us, event | category | flops | bytes accessed | tf_op | source)
XLA Modules:
  0.0 750.5 jit_solution(3505785957954244166)
XLA Ops:
  9.8 30.9 %all_to_all.30 = bf16[8,64,512]{2,1,0:T(8,128)(2,1)} all-to-all(bf16[8,64,512]{2,1,0:T(8,128)(2,1)S(1)} %reshape.545), channel_id=1, replica_groups=mesh['seq'=4,'head'=8] {'head'}, dimensions={0} | all-to-all | bytes 1048576 | tf_op jit(solution)/shard_map/all_to_all | solution.py:117
  41.3 32.0 %all_to_all.31 = bf16[8,64,512]{2,1,0:T(8,128)(2,1)} all-to-all(bf16[8,64,512]{2,1,0:T(8,128)(2,1)S(1)} %reshape.557), channel_id=1, replica_groups=mesh['seq'=4,'head'=8] {'head'}, dimensions={0} | all-to-all | bytes 1048576 | tf_op jit(solution)/shard_map/all_to_all | solution.py:117
  84.7 13.7 %all-gather = bf16[32,55,64]{2,0,1:T(8,128)(2,1)S(1)} all-gather(bf16[8,55,64]{2,0,1:T(8,128)(2,1)S(1)} %copy.437), channel_id=2, replica_groups=mesh['seq'=4,'head'=8] {'seq'}, dimensions={0}, use_global_device_ids=true | all-gather | bytes 281600 | tf_op jit(solution)/shard_map/all_gather | solution.py:118
  106.0 11.3 %all-gather.15.cloned.1.call-done = bf16[32,64,512]{2,1,0:T(8,128)(2,1)} async-done(((bf16[8,64,512]{2,1,0:T(8,128)(2,1)}), bf16[32,64,512]{2,1,0:T(8,128)(2,1)}) %all-gather.15.cloned.1.call-update) | async-done | bytes 2097168 | tf_op jit(solution)/shard_map/all_gather | solution.py:118
  131.9 25.1 %all-gather.17.cloned.1.call-done = bf16[32,64,512]{2,1,0:T(8,128)(2,1)} async-done(((bf16[8,64,512]{2,1,0:T(8,128)(2,1)}), bf16[32,64,512]{2,1,0:T(8,128)(2,1)}) %all-gather.17.cloned.1.call-update) | async-done | bytes 2097168 | tf_op jit(solution)/shard_map/all_gather | solution.py:118
  157.0 6.7 fusion.123
  166.6 14.7 %all_gather.35 = bf16[2,256,512]{2,1,0:T(8,128)(2,1)S(1)} all-gather(bf16[2,32,512]{2,1,0:T(8,128)(2,1)S(1)} %get-tuple-element.78), channel_id=1, replica_groups=mesh['seq'=4,'head'=8] {'head'}, dimensions={1}, use_global_device_ids=true | all-gather | bytes 589824 | tf_op jit(solution)/shard_map/all_gather | solution.py:188
  207.8 15.3 %collective-permute-done.2 = bf16[2,8,136,64]{2,3,1,0:T(8,128)(2,1)} collective-permute-done((bf16[2,8,136,64]{2,3,1,0:T(8,128)(2,1)}, bf16[2,8,136,64]{2,3,1,0:T(8,128)(2,1)}, u32[]{:S(2)}, u32[]{:S(2)}) %collective-permute-start.2) | collective-permute-done | bytes 278560 | tf_op jit(solution)/shard_map/ppermute | solution.py:51
  242.6 8.9 %multiply_reduce_fusion.10 = (f32[2,512]{1,0:T(2,128)S(1)}, f32[2,512]{1,0:T(2,128)S(1)}, f32[2,512,512]{1,2,0:T(8,128)}, f32[2,512,512]{1,2,0:T(8,128)}) fusion(f32[512]{0:T(512)S(1)} %bitcast.406, f32[2,512,512]{1,2,0:T(8,128)} %reshape.588, f32[2,512,512]{1,2,0:T(8,128)} %fusion.123, bf16[2,512,2048]{2,1,0:T(8,128)(2,1)} %all-gather.11.cloned.1.call-done, ...), kind=kOutput, calls=%fused_computation.60 | convolution fusion | flops 2152724480 | bytes 14690304 | tf_op jit(solution)/shard_map/mtd,kd->mtk/dot_general | solution.py:22
  251.6 15.4 %psum.35 = f32[2,2,512]{2,1,0:T(2,128)S(1)} all-reduce(f32[2,2,512]{2,1,0:T(2,128)S(1)} %pad_maximum_fusion.12), channel_id=1, replica_groups=mesh['seq'=4,'head'=8] {'head'}, use_global_device_ids=true, to_apply=%region_9.10 | all-reduce | flops 2048 | bytes 16384 | tf_op jit(solution)/shard_map/psum | solution.py:240
  285.4 19.6 %collective-permute-done.5 = bf16[2,8,136,64]{2,3,1,0:T(8,128)(2,1)S(1)} collective-permute-done((bf16[2,8,136,64]{2,3,1,0:T(8,128)(2,1)S(1)}, bf16[2,8,136,64]{2,3,1,0:T(8,128)(2,1)S(1)}, u32[]{:S(2)}, u32[]{:S(2)}) %collective-permute-start.5) | collective-permute-done | bytes 278560 | tf_op jit(solution)/shard_map/ppermute | solution.py:51
  313.7 5.9 fusion.12
  369.2 6.4 bitcast_convert_fusion.2
  387.5 6.7 bitcast_convert_fusion.1
  395.8 5.9 bitcast_convert_fusion
  415.0 6.1 convolution_convert_fusion
  422.4 8.2 %all_to_all.32 = bf16[8,2,1280]{2,1,0:T(2,128)(2,1)S(1)} all-to-all(bf16[8,2,1280]{2,1,0:T(2,128)(2,1)S(1)} %reshape.687), channel_id=1, replica_groups=mesh['seq'=4,'head'=8] {'head'}, dimensions={0} | all-to-all | bytes 81920 | tf_op jit(solution)/shard_map/all_to_all | solution.py:342
  436.4 13.5 %all-to-all-done.3 = bf16[8,64,512]{2,1,0:T(8,128)(2,1)S(1)} async-done(((bf16[8,64,512]{2,1,0:T(8,128)(2,1)}), bf16[8,64,512]{2,1,0:T(8,128)(2,1)S(1)}, u32[]{:S(2)}, u32[]{:S(2)}) %all-to-all-start.3) | async-done | bytes 524320 | tf_op jit(solution)/shard_map/all_to_all | solution.py:342
  449.9 19.1 %reduce-scatter.16.cloned.1.call-done = bf16[512,512]{1,0:T(8,128)(2,1)} async-done(((bf16[2048,512]{1,0:T(8,128)(2,1)}), bf16[512,512]{1,0:T(8,128)(2,1)}) %reduce-scatter.16.cloned.1.call-update) | async-done | bytes 524304 | tf_op jit(solution)/shard_map/reduce_scatter | solution.py:341
  473.7 40.7 %all-reduce.9 = (f32[2048]{0:T(1024)S(1)}, f32[3,64]{1,0:T(4,128)S(1)}, f32[4096]{0:T(1024)S(1)}) all-reduce(f32[2048]{0:T(1024)S(1)} %get-tuple-element.80, f32[3,64]{1,0:T(4,128)S(1)} %reshape.581, f32[4096]{0:T(1024)S(1)} %bitcast.381), channel_id=1, replica_groups=mesh['seq'=4,'head'=8] {'seq','head'}, use_global_device_ids=true, to_apply=%region_22.23 | all-reduce | flops 6336 | bytes 50688 | tf_op jit(solution)/shard_map/psum | solution.py:384
  516.2 81.6 %all-reduce.12.cloned.1.call-done = f32[5,4352]{1,0:T(8,128)} async-done(((f32[5,4352]{1,0:T(8,128)}), f32[5,4352]{1,0:T(8,128)}) %all-reduce.12.cloned.1.call-update) | async-done | bytes 87056 | tf_op jit(solution)/shard_map/psum | solution.py:384
  600.9 37.4 %reduce-scatter.20.cloned.1.call-done = bf16[128,2048]{1,0:T(8,128)(2,1)} async-done(((bf16[512,2048]{1,0:T(8,128)(2,1)}), bf16[128,2048]{1,0:T(8,128)(2,1)}) %reduce-scatter.20.cloned.1.call-update) | async-done | bytes 524304 | tf_op jit(solution)/shard_map/reduce_scatter | solution.py:361
  645.2 45.5 %reduce-scatter.12.cloned.1.call-done = bf16[2,64,2048]{2,1,0:T(8,128)(2,1)} async-done(((bf16[2,512,2048]{2,1,0:T(8,128)(2,1)}), bf16[2,64,2048]{2,1,0:T(8,128)(2,1)}) %reduce-scatter.12.cloned.1.call-update) | async-done | bytes 524304 | tf_op jit(solution)/shard_map/reduce_scatter | solution.py:329
  692.1 49.2 %reduce-scatter.8.cloned.1.call-done = bf16[2,64,2048]{2,1,0:T(8,128)(2,1)} async-done(((bf16[2,512,2048]{2,1,0:T(8,128)(2,1)}), bf16[2,64,2048]{2,1,0:T(8,128)(2,1)}) %reduce-scatter.8.cloned.1.call-update) | async-done | bytes 524304 | tf_op jit(solution)/shard_map/reduce_scatter | solution.py:244
  (542 shorter events, 214.8 us)
Async XLA Ops:
  7.2 95.4 %all-gather.9.cloned.1.call-start = ((), (), s32[]{:S(2)}) async-start(), calls=%async_computation.13 | async-start | bytes 4718592 | tf_op jit(solution)/shard_map/all_gather | solution.py:153
  7.9 109.4 %all-gather.15.cloned.1.call-start = ((), (), s32[]{:S(2)}) async-start(), calls=%async_computation.24 | async-start | bytes 2621440 | tf_op jit(solution)/shard_map/all_gather | solution.py:118
  40.6 116.4 %all-gather.17.cloned.1.call-start = ((), (), s32[]{:S(2)}) async-start(), calls=%async_computation.25 | async-start | bytes 2621440 | tf_op jit(solution)/shard_map/all_gather | solution.py:118
  73.3 167.8 %all-gather.13.cloned.1.call-start = ((), (), s32[]{:S(2)}) async-start(), calls=%async_computation.15 | async-start | bytes 2621440 | tf_op jit(solution)/shard_map/all_gather | solution.py:148
  75.3 9.2 %all-to-all-start = ((bf16[8,2,1760]{2,1,0:T(2,128)(2,1)}), bf16[8,2,1760]{2,1,0:T(2,128)(2,1)S(1)}, u32[]{:S(2)}, u32[]{:S(2)}) async-start(bf16[8,2,1760]{2,1,0:T(2,128)(2,1)} %reshape.685), calls=%async_computation | async-start | bytes 114688 | tf_op jit(solution)/shard_map/all_to_all | solution.py:117
  78.7 163.9 %all-gather.11.cloned.1.call-start = ((), (), s32[]{:S(2)}) async-start(), calls=%async_computation.14 | async-start | bytes 4718592 | tf_op jit(solution)/shard_map/all_gather | solution.py:154
  79.3 277.7 %reduce-scatter.10.cloned.1.call-start = ((), (), s32[]{:S(2)}) async-start(), calls=%async_computation.17 | async-start | bytes 1179648 | tf_op jit(solution)/shard_map/reduce_scatter | solution.py:291
  127.8 37.8 %collective-permute-start = (bf16[2,3,544]{1,2,0:T(8,128)(2,1)S(1)}, bf16[2,3,544]{1,2,0:T(8,128)(2,1)S(1)}, u32[]{:S(2)}, u32[]{:S(2)}) collective-permute-start(bf16[2,3,544]{1,2,0:T(8,128)(2,1)S(1)} %pad_maximum_fusion.5), channel_id=1, source_target_pairs={{0,8},{8,16},{16,24},{1,9},{9,17},{17,25},{2,10},{10,18},{18,26},{... | collective-permute-start | bytes 19592 | tf_op jit(solution)/shard_map/ppermute | solution.py:176
  194.4 31.3 %collective-permute-start.3 = (bf16[2,8,136,64]{2,3,1,0:T(8,128)(2,1)}, bf16[2,8,136,64]{2,3,1,0:T(8,128)(2,1)}, u32[]{:S(2)}, u32[]{:S(2)}) collective-permute-start(bf16[2,8,136,64]{2,3,1,0:T(8,128)(2,1)} %pad_maximum_fusion.4), channel_id=1, source_target_pairs={{0,24},{1,25},{2,26},{3,27},{4,28},{5,29},{6,30},{7,31}} | collective-permute-start | bytes 835592 | tf_op jit(solution)/shard_map/ppermute | solution.py:51
  198.6 24.5 %collective-permute-start.2 = (bf16[2,8,136,64]{2,3,1,0:T(8,128)(2,1)}, bf16[2,8,136,64]{2,3,1,0:T(8,128)(2,1)}, u32[]{:S(2)}, u32[]{:S(2)}) collective-permute-start(bf16[2,8,136,64]{2,3,1,0:T(8,128)(2,1)} %pad_maximum_fusion.4), channel_id=1, source_target_pairs={{0,16},{8,24},{1,17},{9,25},{2,18},{10,26},{3,19},{11,27},{4,20},{... | collective-permute-start | bytes 835592 | tf_op jit(solution)/shard_map/ppermute | solution.py:51
  200.7 23.6 %collective-permute-start.1 = (bf16[2,8,136,64]{2,3,1,0:T(8,128)(2,1)}, bf16[2,8,136,64]{2,3,1,0:T(8,128)(2,1)}, u32[]{:S(2)}, u32[]{:S(2)}) collective-permute-start(bf16[2,8,136,64]{2,3,1,0:T(8,128)(2,1)} %pad_maximum_fusion.4), channel_id=1, source_target_pairs={{0,8},{8,16},{16,24},{1,9},{9,17},{17,25},{2,10},{10,18},{18,26},{... | collective-permute-start | bytes 835592 | tf_op jit(solution)/shard_map/ppermute | solution.py:51
  278.1 27.4 %collective-permute-start.6 = (bf16[2,8,136,64]{2,3,1,0:T(8,128)(2,1)S(1)}, bf16[2,8,136,64]{2,3,1,0:T(8,128)(2,1)S(1)}, u32[]{:S(2)}, u32[]{:S(2)}) collective-permute-start(bf16[2,8,136,64]{2,3,1,0:T(8,128)(2,1)S(1)} %pad_maximum_fusion.3), channel_id=1, source_target_pairs={{24,0},{25,1},{26,2},{27,3},{28,4},{29,5},{30,6},{31,7}} | collective-permute-start | bytes 835592 | tf_op jit(solution)/shard_map/ppermute | solution.py:51
  279.7 25.3 %collective-permute-start.5 = (bf16[2,8,136,64]{2,3,1,0:T(8,128)(2,1)S(1)}, bf16[2,8,136,64]{2,3,1,0:T(8,128)(2,1)S(1)}, u32[]{:S(2)}, u32[]{:S(2)}) collective-permute-start(bf16[2,8,136,64]{2,3,1,0:T(8,128)(2,1)S(1)} %pad_maximum_fusion.3), channel_id=1, source_target_pairs={{16,0},{24,8},{17,1},{25,9},{18,2},{26,10},{19,3},{27,11},{20,4},{... | collective-permute-start | bytes 835592 | tf_op jit(solution)/shard_map/ppermute | solution.py:51
  281.0 24.1 %collective-permute-start.4 = (bf16[2,8,136,64]{2,3,1,0:T(8,128)(2,1)S(1)}, bf16[2,8,136,64]{2,3,1,0:T(8,128)(2,1)S(1)}, u32[]{:S(2)}, u32[]{:S(2)}) collective-permute-start(bf16[2,8,136,64]{2,3,1,0:T(8,128)(2,1)S(1)} %pad_maximum_fusion.3), channel_id=1, source_target_pairs={{8,0},{16,8},{24,16},{9,1},{17,9},{25,17},{10,2},{18,10},{26,18},{... | collective-permute-start | bytes 835592 | tf_op jit(solution)/shard_map/ppermute | solution.py:51
  327.0 94.2 %reduce-scatter.18.cloned.1.call-start = ((), (), s32[]{:S(2)}) async-start(), calls=%async_computation.21 | async-start | bytes 204800 | tf_op jit(solution)/shard_map/reduce_scatter | solution.py:341
  358.6 5.6 collective-permute-start.7
  369.1 61.5 %reduce-scatter.14.cloned.1.call-start = ((), (), s32[]{:S(2)}) async-start(), calls=%async_computation.19 | async-start | bytes 2621440 | tf_op jit(solution)/shard_map/reduce_scatter | solution.py:341
  375.6 93.4 %reduce-scatter.16.cloned.1.call-start = ((), (), s32[]{:S(2)}) async-start(), calls=%async_computation.20 | async-start | bytes 2621440 | tf_op jit(solution)/shard_map/reduce_scatter | solution.py:341
  394.2 203.6 %all-reduce.12.cloned.1.call-start = ((), (), s32[]{:S(2)}) async-start(), calls=%async_computation.22 | async-start | bytes 278528 | tf_op jit(solution)/shard_map/psum | solution.py:384
  395.5 242.9 %reduce-scatter.20.cloned.1.call-start = ((), (), s32[]{:S(2)}) async-start(), calls=%async_computation.23 | async-start | bytes 2621440 | tf_op jit(solution)/shard_map/reduce_scatter | solution.py:361
  401.8 288.9 %reduce-scatter.12.cloned.1.call-start = ((), (), s32[]{:S(2)}) async-start(), calls=%async_computation.18 | async-start | bytes 4718592 | tf_op jit(solution)/shard_map/reduce_scatter | solution.py:329
  413.4 327.8 %reduce-scatter.8.cloned.1.call-start = ((), (), s32[]{:S(2)}) async-start(), calls=%async_computation.16 | async-start | bytes 4718592 | tf_op jit(solution)/shard_map/reduce_scatter | solution.py:244
  430.6 19.3 %all-to-all-start.3 = ((bf16[8,64,512]{2,1,0:T(8,128)(2,1)}), bf16[8,64,512]{2,1,0:T(8,128)(2,1)S(1)}, u32[]{:S(2)}, u32[]{:S(2)}) async-start(bf16[8,64,512]{2,1,0:T(8,128)(2,1)} %bitcast.356), calls=%async_computation.7 | async-start | bytes 1048576 | tf_op jit(solution)/shard_map/all_to_all | solution.py:342
  468.9 173.1 %all-to-all-start.4 = ((bf16[8,64,512]{2,1,0:T(8,128)(2,1)}), bf16[8,64,512]{2,1,0:T(8,128)(2,1)S(1)}, u32[]{:S(2)}, u32[]{:S(2)}) async-start(bf16[8,64,512]{2,1,0:T(8,128)(2,1)} %bitcast.355), calls=%async_computation.9 | async-start | bytes 1048576 | tf_op jit(solution)/shard_map/all_to_all | solution.py:342
  (118 other events, 1506.3 us)
Sparse Core Ops, SparseCore 0:
  9.6 68.2 all-gather.8
  79.7 37.5 all-gather.14
  119.1 37.7 all-gather.16
  158.7 35.2 all-gather.12
  195.5 47.1 all-gather.10
  327.1 29.8 reduce-scatter.9
  369.2 22.4 reduce-scatter.17
  394.7 35.1 reduce-scatter.13
  433.7 35.1 reduce-scatter.15
  474.9 122.8 all-reduce.11
  600.8 37.5 reduce-scatter.19
  640.6 49.9 reduce-scatter.11
  693.1 48.1 reduce-scatter.7
